TPU v7x, 512 devices: a whole 4x8x8 slice. The times are simulated.
512 devices in a mesh: branch: 16 (over y, core), leaf: 32 (over z, x).
Axes of the slice: x: 4, y: 8, z: 8, core: 2. Of those that a mesh axis runs over, the one named last changes fastest.
Arguments:
- vectors: bfloat16 [32, 786432], P(None, ('branch', 'leaf')), may hold values from -6 to 6
- leaf_cluster_bases: bfloat16 [3072, 256, 128], P(('branch', 'leaf')), may hold values from -0.375 to 0.375
- transfers: bfloat16 [3072, 128, 128], P(('branch', 'leaf')), may hold values from -0.5 to 0.5
- parents: int32 [3072], P(('branch', 'leaf')), may hold values from 0 to 1023, as said below
- leaf_pairs: int32 [16384, 2], P(('branch', 'leaf')), may hold values from 0 to 3071, as said below
- live_pairs: int32 [512], P(('branch', 'leaf')), may hold values from 8 to 32
- couplings: bfloat16 [16384, 128, 128], P(('branch', 'leaf')), may hold values from -0.25 to 0.25
- upper_pairs: int32 [2048, 2], P(('branch', 'leaf')), may hold values from 0 to 1023, as said below
- upper_coupling_matrices: bfloat16 [2048, 128, 128], P(('branch', 'leaf')), may hold values from -0.1875 to 0.1875
- self_blocks: bfloat16 [3072, 256, 256], P(('branch', 'leaf')), may hold values from -0.375 to 0.375
- near_pairs: int32 [4096, 2], P(('branch', 'leaf')), may hold values from 0 to 3071, as said below
- near_blocks: bfloat16 [4096, 256, 256], P(('branch', 'leaf')), may hold values from -0.25 to 0.25
Outputs:
- product: bfloat16 [32, 786432], P(None, ('branch', 'leaf'))
Inputs may be any that keep to these rules, and one draw needn't show every extreme that they name: parents[c] // 2 == c // 6: a leaf's parent lies on the leaf's device. `leaf_pairs`: slot k is held by device k // 32 (devices counted branch first). Its first cluster lies on that device, its second on another device of the same branch; at most 2 of one device's slots have their second cluster on one given device. `upper_pairs`: upper pair k is held by device k // 4; its first cluster lies on that device, its second on a device of another branch with the same leaf index. `near_pairs`: near pair k is held by device k // 8; both its clusters lie on that device and differ.
All inputs are finite; a program needn't handle non-finite values.
Results may differ from a plain program's by a relative error of at most 0.0052.
Values may be sent and summed in bfloat16 or wider, within the bound.
A program may use at most 64 MiB of HBM per device.

v0:
```python
import jax
import jax.numpy as jnp
from jax import lax
from jax.sharding import PartitionSpec as P

CPD = 6
P1D = 2


def select_rows(indices, row_count):
    targets = jnp.arange(row_count, dtype=jnp.int32)
    return (indices[None, :] == targets[:, None]).astype(jnp.float32)


def add_rows(pick_rows, terms):
    return jnp.einsum("rp,pvk->rvk", pick_rows, terms, precision=lax.Precision.HIGHEST)


def couple(partner, own_coeffs, matrices, weight):
    to_first = jnp.einsum("pvk,pkj->pvj", partner, matrices, preferred_element_type=jnp.float32)
    to_second = jnp.einsum("pvj,pkj->pvk", own_coeffs, matrices, preferred_element_type=jnp.float32)
    return (to_first * weight, to_second * weight)


def on_device(
    vectors,
    leaf_cluster_bases,
    transfers,
    parents,
    leaf_pairs,
    live_pairs,
    couplings,
    upper_pairs,
    upper_coupling_matrices,
    self_blocks,
    near_pairs,
    near_blocks,
):
    leaf_count = leaf_cluster_bases.shape[0]
    vec_count = vectors.shape[0]
    leaf_size = leaf_cluster_bases.shape[1]
    pair_count = leaf_pairs.shape[0]
    cluster_group_size = lax.axis_size("leaf")
    vector_columns = vectors.reshape(vec_count, leaf_count, leaf_size)
    leaf_coefficients = jnp.einsum(
        "jif,ifs->ijs", vector_columns, leaf_cluster_bases, preferred_element_type=jnp.float32
    ).astype(jnp.bfloat16)
    lifted = jnp.einsum(
        "cvk,ckj->cvj", leaf_coefficients, transfers, preferred_element_type=jnp.float32
    )
    parent_local = parents % P1D
    parent_coeffs = add_rows(select_rows(parent_local, P1D), lifted).astype(jnp.bfloat16)
    first_local = leaf_pairs[:, 0] % CPD
    second_global = leaf_pairs[:, 1]
    second_in_branch = second_global % (cluster_group_size * CPD)
    live_weight = (jnp.arange(pair_count, dtype=jnp.int32) < live_pairs[0]).astype(jnp.float32)[
        :, None, None
    ]
    own_coeffs = leaf_coefficients[first_local]
    branch_coeffs = lax.all_gather(leaf_coefficients, "leaf", axis=0, tiled=True)
    partner = branch_coeffs[second_in_branch]
    to_first, to_second = couple(partner, own_coeffs, couplings, live_weight)
    returned = lax.psum_scatter(
        add_rows(select_rows(second_in_branch, leaf_count * lax.axis_size("leaf")), to_second),
        "leaf",
        scatter_dimension=0,
        tiled=True,
    )
    leaf_field = add_rows(select_rows(first_local, leaf_count), to_first) + returned
    upper_all = lax.all_gather(parent_coeffs, "branch", axis=0, tiled=True)
    upper_first = upper_pairs[:, 0] % P1D
    upper_second = upper_pairs[:, 1]
    upper_device = upper_second // P1D
    upper_row = upper_device // cluster_group_size * P1D + upper_second % P1D
    upper_weight = jnp.ones((upper_pairs.shape[0], 1, 1), jnp.float32)
    upper_to_first, upper_to_second = couple(
        upper_all[upper_row], parent_coeffs[upper_first], upper_coupling_matrices, upper_weight
    )
    upper_returned = lax.psum_scatter(
        add_rows(select_rows(upper_row, P1D * lax.axis_size("branch")), upper_to_second),
        "branch",
        scatter_dimension=0,
        tiled=True,
    )
    parent_field = (
        add_rows(select_rows(upper_first, P1D), upper_to_first) + upper_returned
    ).astype(jnp.bfloat16)
    lowered = jnp.einsum(
        "cvj,ckj->cvk", parent_field[parent_local], transfers, preferred_element_type=jnp.float32
    )
    total_leaf_count = (leaf_field + lowered).astype(jnp.bfloat16)
    near_first = near_pairs[:, 0] % CPD
    near_second = near_pairs[:, 1] % CPD
    first_cols = jnp.take(vector_columns, near_first, axis=1)
    second_cols = jnp.take(vector_columns, near_second, axis=1)
    near_to_first = jnp.einsum(
        "vnl,nlm->nvm", second_cols, near_blocks, preferred_element_type=jnp.float32
    )
    near_to_second = jnp.einsum(
        "vnm,nlm->nvl", first_cols, near_blocks, preferred_element_type=jnp.float32
    )
    nearby_field_blocks = jnp.einsum(
        "vcl,clm->cvm", vector_columns, self_blocks, preferred_element_type=jnp.float32
    )
    nearby_field_blocks = nearby_field_blocks + add_rows(
        select_rows(near_first, leaf_count), near_to_first
    )
    nearby_field_blocks = nearby_field_blocks + add_rows(
        select_rows(near_second, leaf_count), near_to_second
    )
    product_output = nearby_field_blocks + jnp.einsum(
        "gbj,gxj->gbx", total_leaf_count, leaf_cluster_bases, preferred_element_type=jnp.float32
    )
    return (
        jnp.transpose(product_output, (1, 0, 2))
        .reshape(vec_count, leaf_count * leaf_size)
        .astype(jnp.bfloat16)
    )


def solution(mesh):
    return jax.shard_map(
        on_device,
        mesh=mesh,
        in_specs=(
            P(None, ("branch", "leaf")),
            P(("branch", "leaf"), None, None),
            P(("branch", "leaf"), None, None),
            P(("branch", "leaf")),
            P(("branch", "leaf"), None),
            P(("branch", "leaf")),
            P(("branch", "leaf"), None, None),
            P(("branch", "leaf"), None),
            P(("branch", "leaf"), None, None),
            P(("branch", "leaf"), None, None),
            P(("branch", "leaf"), None),
            P(("branch", "leaf"), None, None),
        ),
        out_specs=P(None, ("branch", "leaf")),
        check_vma=False,
    )
```

profile of v0, /device:TPU:16, one launch (start us, length us, event | category | flops | bytes accessed | tf_op | source)
XLA Modules:
  0.0 318.7 jit_solution(17716666005419100217)
XLA Ops:
  7.4 0.0 copy-start
  7.4 0.0 copy-start.8
  7.4 0.0 reduce-scatter.5.cloned.1.call-start
  7.4 0.8 fusion.56
  8.2 0.8 and_select_fusion.8
  9.0 0.7 compare_select_fusion.2
  9.6 1.2 convolution_convert_fusion
  10.9 0.0 copy-start.2
  10.9 1.1 fusion.62
  12.0 0.2 convolution_convert_fusion.1
  12.3 0.6 gather_fusion.3
  12.8 1.1 fusion.64
  13.9 0.5 fusion.21
  14.4 1.1 copy.104
  15.5 0.0 reduce-scatter.5.cloned.1.call-update
  15.6 0.0 all-gather.2.cloned.1.call-start
  15.6 0.0 copy-done.2
  15.6 0.5 all-gather.2.cloned.1.call-update
  16.1 0.0 reduce-scatter.3.cloned.1.call-start
  16.2 0.0 copy-done.8
  16.2 1.4 gather_fusion.1
  18.3 0.0 copy-start.9
  18.3 0.5 and_select_fusion.12
  18.8 0.0 copy-done
  18.8 0.6 convolution_multiply_fusion
  19.5 1.5 fusion.4
  21.0 3.5 %copy.97 = f32[192,32,128]{2,1,0:T(8,128)} copy(f32[192,32,128]{2,0,1:T(8,128)S(1)} %fusion.4) | data formatting | bytes 6291456 | tf_op jit(solution)/shard_map/rp,pvk->rvk/dot_general | solution.py:16
  24.5 0.0 copy-done.9
  24.5 0.0 copy-start.4
  24.5 0.0 copy-start.10
  24.5 0.0 copy-start.7
  24.5 0.0 copy-start.1
  24.5 0.0 reduce-scatter.3.cloned.1.call-update
  24.5 0.8 copy-done.4
  25.4 0.0 copy-start.5
  25.4 0.0 copy-done.10
  25.5 0.6 gather_fusion.5
  26.0 0.6 gather_fusion.6
  26.6 19.3 %all_gather.7 = bf16[32,32,128]{2,1,0:T(8,128)(2,1)} all-gather(bf16[2,32,128]{2,1,0:T(8,128)(2,1)S(1)} %copy.100), channel_id=1, replica_groups=mesh['branch'=16,'leaf'=32] {'branch'}, dimensions={0}, use_global_device_ids=true | all-gather | bytes 278528 | tf_op jit(solution)/shard_map/all_gather | solution.py:70
  46.0 1.5 gather_fusion.2
  47.5 0.0 copy-done.7
  47.5 0.1 fusion.63
  47.7 0.2 fusion.23
  47.9 0.0 copy-done.1
  47.9 0.3 fusion.14
  48.2 0.4 fusion.10
  48.6 0.0 copy-start.3
  48.6 0.4 fusion.12
  49.1 0.0 copy-start.6
  49.1 0.4 fusion.8
  49.5 0.0 copy-done.5
  49.5 0.3 fusion
  49.8 25.1 %reduce-scatter.5.cloned.1.call-done = f32[2,32,128]{2,1,0:T(8,128)} async-done(((f32[32,32,128]{2,1,0:T(8,128)}), f32[2,32,128]{2,1,0:T(8,128)}) %reduce-scatter.5.cloned.1.call-update) | async-done | bytes 32784 | tf_op jit(solution)/shard_map/reduce_scatter | solution.py:79
  74.9 0.8 fusion.27
  75.6 0.6 gather_fusion.4
  76.2 31.0 %all-gather.2.cloned.1.call-done = bf16[192,32,128]{2,1,0:T(8,128)(2,1)} async-done(((bf16[6,32,128]{2,1,0:T(8,128)(2,1)}), bf16[192,32,128]{2,1,0:T(8,128)(2,1)}) %all-gather.2.cloned.1.call-update) | async-done | bytes 1572880 | tf_op jit(solution)/shard_map/all_gather | solution.py:60
  107.2 2.0 gather_fusion
  109.2 1.0 convolution_multiply_fusion.1
  110.2 1.2 fusion.6
  111.4 198.0 %reduce-scatter.3.cloned.1.call-done = f32[6,32,128]{2,1,0:T(8,128)} async-done(((f32[192,32,128]{2,1,0:T(8,128)}), f32[6,32,128]{2,1,0:T(8,128)}) %reduce-scatter.3.cloned.1.call-update) | async-done | bytes 98320 | tf_op jit(solution)/shard_map/reduce_scatter | solution.py:63
  309.3 0.0 copy-done.3
  309.3 0.0 copy-done.6
  309.3 1.2 fusion.2
  310.6 0.6 copy.108
  (13 shorter events, 0.1 us)
Async XLA Ops:
  7.4 11.5 %copy-start = (bf16[32,128,128]{2,1,0:T(8,128)(2,1)S(1)}, bf16[32,128,128]{2,1,0:T(8,128)(2,1)}, u32[]{:S(2)}) copy-start(bf16[32,128,128]{2,1,0:T(8,128)(2,1)} %param.20) | copy-start | bytes 3145732
  7.4 8.8 %copy-start.8 = (s32[32,2]{0,1:T(2,128)S(1)}, s32[32,2]{0,1:T(2,128)}, u32[]{:S(2)}) copy-start(s32[32,2]{0,1:T(2,128)} %param.18) | copy-start | bytes 772
  7.4 67.5 %reduce-scatter.5.cloned.1.call-start = ((), (), s32[]{:S(2)}) async-start(), calls=%async_computation.4 | async-start | bytes 557056 | tf_op jit(solution)/shard_map/reduce_scatter | solution.py:79
  10.9 4.7 %copy-start.2 = (bf16[6,32,128]{2,1,0:T(8,128)(2,1)}, bf16[6,32,128]{2,1,0:T(8,128)(2,1)S(1)}, u32[]{:S(2)}) copy-start(bf16[6,32,128]{2,1,0:T(8,128)(2,1)S(1)} %convolution_convert_fusion) | copy-start | bytes 147460
  15.6 91.6 %all-gather.2.cloned.1.call-start = ((), (), s32[]{:S(2)}) async-start(), calls=%async_computation.2 | async-start | bytes 1622016 | tf_op jit(solution)/shard_map/all_gather | solution.py:60
  16.1 293.2 %reduce-scatter.3.cloned.1.call-start = ((), (), s32[]{:S(2)}) async-start(), calls=%async_computation.3 | async-start | bytes 3244032 | tf_op jit(solution)/shard_map/reduce_scatter | solution.py:63
  18.3 6.2 %copy-start.9 = (f32[32]{0:T(128)}, f32[32]{0:T(128)S(1)}, u32[]{:S(2)}) copy-start(f32[32]{0:T(128)S(1)} %compare_convert_fusion) | copy-start | bytes 388
  24.5 0.9 copy-start.4
  24.5 0.9 copy-start.10
  24.5 23.0 %copy-start.7 = (bf16[4,128,128]{2,1,0:T(8,128)(2,1)S(1)}, bf16[4,128,128]{2,1,0:T(8,128)(2,1)}, u32[]{:S(2)}) copy-start(bf16[4,128,128]{2,1,0:T(8,128)(2,1)} %param.22) | copy-start | bytes 393220
  24.5 23.4 %copy-start.1 = (bf16[8,256,256]{2,1,0:T(8,128)(2,1)S(1)}, bf16[8,256,256]{2,1,0:T(8,128)(2,1)}, u32[]{:S(2)}) copy-start(bf16[8,256,256]{2,1,0:T(8,128)(2,1)} %param.25) | copy-start | bytes 3145732
  25.4 24.1 %copy-start.5 = (bf16[6,256,256]{2,1,0:T(8,128)(2,1)S(1)}, bf16[6,256,256]{2,1,0:T(8,128)(2,1)}, u32[]{:S(2)}) copy-start(bf16[6,256,256]{2,1,0:T(8,128)(2,1)} %param.23) | copy-start | bytes 2359300
  48.6 260.7 %copy-start.3 = (bf16[6,256,128]{2,1,0:T(8,128)(2,1)S(1)}, bf16[6,256,128]{2,1,0:T(8,128)(2,1)}, u32[]{:S(2)}) copy-start(bf16[6,256,128]{2,1,0:T(8,128)(2,1)} %param.15) | copy-start | bytes 1179652
  49.1 260.3 %copy-start.6 = (bf16[6,128,128]{2,1,0:T(8,128)(2,1)S(1)}, bf16[6,128,128]{2,1,0:T(8,128)(2,1)}, u32[]{:S(2)}) copy-start(bf16[6,128,128]{2,1,0:T(8,128)(2,1)} %param.16) | copy-start | bytes 589828
Sparse Core Ops, SparseCore 0:
  15.7 59.1 reduce-scatter.4
  80.0 229.3 reduce-scatter.2
Sparse Core Ops, SparseCore 1:
  19.2 87.9 all-gather.1
where the time goes:
time: 319 us
  waiting for transfers between devices  255 us (80%)
  blocking collectives  19.3 us (6%)
  between operations  15.8 us (5%)
  local copies, waits for them, and re-layouts  13.3 us (4%)
  matrix products  12 us (4%)
  other arithmetic  3.64 us (1%)
    reduce_scatter x1, waiting for transfers between devices, on_device(): lax.psum_scatter(add_rows(select_rows(second_in_branch, leaf_count * lax....  198 us
    all_gather x1, waiting for transfers between devices, on_device(): lax.all_gather(leaf_coefficients, 'leaf', axis=0, tiled=True)  31 us
    reduce_scatter x1, waiting for transfers between devices, on_device(): lax.psum_scatter(add_rows(select_rows(upper_row, P1D * lax.axis_size('bra...  25.1 us
    all_gather x1, blocking collectives, on_device(): upper_all = lax.all_gather(parent_coeffs, 'branch', axis=0, tiled=True)  19.3 us
  transfers between devices with their start and end apart: 3, of which 3 were waited for; matrix products, arithmetic and copies ran while one was open for 6% of the time, Pallas kernels for 0%

commit v1 on v0

v1 whole, which is shorter than its diff:
```python
import jax
import jax.numpy as jnp
from jax import lax
from jax.experimental import pallas as pl
from jax.experimental.pallas import tpu as pltpu
from jax.sharding import PartitionSpec as P

CPD = 6
P1D = 2
CORES = 2
XDIM = 4
MOST = 2
LANES = 128
FAR = 1000
MESH = pl.DeviceIdType.MESH
F32 = jnp.float32
BF16 = jnp.bfloat16
UNROLL = 8


def dot_nn(a, b):
    return jnp.dot(a, b, preferred_element_type=F32)


def dot_nt(a, b):
    return lax.dot_general(a, b, (((1,), (1,)), ((), ())), preferred_element_type=F32)


def make_kernel(yd, zd):
    cd, xd = CORES, XDIM
    per_x = zd * MOST
    half = zd // 2

    def zi_of(dz):
        dz %= zd
        if dz == 0:
            return 0
        return 2 * dz - 1 if dz <= half else 2 * (zd - dz)

    dz_of = [0] * zd
    for d in range(zd):
        dz_of[zi_of(d)] = d
    groups = [[0]] + [[2 * h - 1, 2 * h] for h in range(1, half)] + [[zd - 1]]
    column = [(dy, dc) for dc in range(cd) for dy in range(yd) if dy or dc]

    def kernel(
        vec_h, bas_h, tra_h, par_s, lp_v, live_s, cou_h, up_s, uco_h, sel_h, np_s, nea_h,
        out_ref,
        vec, bas, tra, cou, uco, sel, nea,
        tab, tabs, p_own, s_a, r_a, s_d, r_d, t_buf, zsend, zrecv, d_own,
        pbuf, u_send, u_recv, pf,
        x3, nacc, lacc,
        lsem, ssem, rsem, *zbuf,
    ):
        b = lax.axis_index("branch")
        l = lax.axis_index("leaf")
        y, c, z, x = b // cd, b % cd, l // xd, l % xd
        pair_count = cou_h.shape[0]
        upper_count = uco_h.shape[0]
        near_count = nea_h.shape[0]
        width = x3.shape[2]

        def at(dy=0, dc=0, dz=0, dx=0):
            yy, cc = (y + dy) % yd, (c + dc) % cd
            zz, xx = (z + dz) % zd, (x + dx) % xd
            return (yy * cd + cc, zz * xd + xx)

        loads = {}
        for i, (name, src, dst) in enumerate(
            (("vec", vec_h, vec), ("bas", bas_h, bas), ("tra", tra_h, tra), ("cou", cou_h, cou),
             ("uco", uco_h, uco), ("sel", sel_h, sel), ("nea", nea_h, nea))
        ):
            loads[name] = pltpu.make_async_copy(src, dst, lsem.at[i])
            loads[name].start()

        barrier = pltpu.get_barrier_semaphore()
        partners = [at(dz=d) for d in range(1, zd)] + [at(dx=d) for d in range(1, xd)]
        partners += [at(dy=dy, dc=dc) for dy, dc in column]
        for device in partners:
            pl.semaphore_signal(barrier, inc=1, device_id=device, device_id_type=MESH)

        count = [0]
        sent = []

        def send(src, dst, device):
            i = count[0]
            count[0] += 1
            copy = pltpu.make_async_remote_copy(
                src_ref=src, dst_ref=dst, send_sem=ssem.at[i], recv_sem=rsem.at[i],
                device_id=device, device_id_type=MESH,
            )
            copy.start()
            sent.append(copy)
            return copy

        def add_where(acc, terms, i):
            for where, term in terms:
                acc = acc + jnp.where(where == i, term, 0.0)
            return acc

        live = live_s[0]
        first = lp_v[0:1, :] % CPD
        second = lp_v[1:2, :] % (zd * xd * CPD)
        owner = (second * 10923) >> 16
        second_c = second - owner * CPD
        oz, ox = owner // xd, owner % xd
        odz = (oz - z + zd) % zd
        odx = (ox - x + xd) % xd
        ozi = jnp.where(odz <= half, 2 * odz - 1, 2 * (zd - odz))
        ozi = jnp.where(odz == 0, 0, ozi)
        peer = odx * zd + ozi
        sub = lax.broadcasted_iota(jnp.int32, (pair_count, pair_count), 0)
        lane = lax.broadcasted_iota(jnp.int32, (pair_count, pair_count), 1)
        eye = sub == lane

        def to_col(row):
            return jnp.sum(jnp.where(eye, row, 0), axis=1, keepdims=True)

        peer_col = to_col(peer)
        rank_col = jnp.sum(
            jnp.where((peer == peer_col) & (lane < sub), 1, 0), axis=1, keepdims=True
        )
        sub_col = lax.broadcasted_iota(jnp.int32, (pair_count, 1), 0)
        pos_col = jnp.where(sub_col < live, peer_col * MOST + rank_col, FAR)
        slot_lane = lax.broadcasted_iota(jnp.int32, (pair_count, LANES), 1)
        hit = pos_col == slot_lane

        def by_slot(col, none):
            return none - jnp.sum(jnp.where(hit, none - col, 0), axis=0, keepdims=True)

        pair_of = by_slot(sub_col, pair_count)
        tab[0] = jnp.zeros_like(tab[0])
        tab[0, 0:1, :] = pair_of
        tab[0, 1:2, :] = by_slot(to_col(second_c), 0)
        tab[0, 2:3, :] = by_slot(to_col(first), CPD)
        tab[0, 3:4, :] = jnp.minimum(pair_of, pair_count - 1)
        tab[0, 4:5, 0:pair_count] = first
        own_tab = pltpu.make_async_copy(tab.at[0], tabs.at[0], lsem.at[7])
        own_tab.start()

        loads["vec"].wait()
        loads["bas"].wait()
        for i in range(CPD):
            xi = vec[:, i * width:(i + 1) * width]
            x3[i] = xi
            zbuf[0][i] = dot_nn(xi, bas[i]).astype(BF16)

        loads["tra"].wait()
        lifted = [(par_s[i] % P1D, dot_nn(zbuf[0][i], tra[i])) for i in range(CPD)]
        for p in range(P1D):
            acc = add_where(jnp.zeros(lifted[0][1].shape, F32), lifted, p).astype(BF16)
            p_own[p] = acc
            pbuf[0, 0, p] = acc

        loads["cou"].wait()
        own_tab.wait()
        t_buf[pair_count] = jnp.zeros_like(t_buf[pair_count])

        def second_body(i, carry):
            for u in range(UNROLL):
                k = i * UNROLL + u
                f = tabs[0, 4, k]
                t_buf[k] = dot_nt(zbuf[0][f], cou[k]).astype(BF16)
            return carry

        lax.fori_loop(0, pair_count // UNROLL, second_body, 0)
        for dx in range(xd):
            buf = r_d if dx == 0 else s_d
            for s in range(dx * per_x, (dx + 1) * per_x):
                buf[s] = t_buf[tabs[0, 0, s]]

        loads["uco"].wait()
        u_first = [up_s[0, k] % P1D for k in range(upper_count)]
        u_row, u_dy, u_dc = [], [], []
        for k in range(upper_count):
            q = up_s[1, k]
            far_b = q // (P1D * zd * xd)
            u_row.append(q % P1D)
            u_dy.append((far_b // cd - y + yd) % yd)
            u_dc.append((far_b % cd - c + cd) % cd)
        u_terms = [
            ((u_dc[k] * yd + u_dy[k]) * P1D + u_row[k], dot_nt(p_own[u_first[k]], uco[k]))
            for k in range(upper_count)
        ]
        for dy, dc in column:
            for p in range(P1D):
                acc = jnp.zeros(u_terms[0][1].shape, F32)
                u_send[dc, dy, p] = add_where(acc, u_terms, (dc * yd + dy) * P1D + p).astype(BF16)

        pl.semaphore_wait(barrier, len(partners))

        def ring(h):
            if h < half:
                src_l, dst_l = zbuf[zi_of(h - 1)], zbuf[zi_of(h)]
                src_r, dst_r = zbuf[zi_of(1 - h)], zbuf[zi_of(-h)]
            else:
                cut = CPD // 2
                src_l, dst_l = zbuf[zi_of(h - 1)].at[0:cut], zbuf[zi_of(h)].at[0:cut]
                src_r, dst_r = zbuf[zi_of(1 - h)].at[cut:CPD], zbuf[zi_of(-h)].at[cut:CPD]
            return [send(src_l, dst_l, at(dz=-1)), send(src_r, dst_r, at(dz=1))]

        def send_slots(src, dst, gi):
            lo, n = groups[gi][0] * MOST, len(groups[gi]) * MOST
            return [
                send(
                    src.at[pl.ds(dx * per_x + lo, n)],
                    dst.at[pl.ds(((-dx) % xd) * per_x + lo, n)],
                    at(dx=dx),
                )
                for dx in range(1, xd)
            ]

        tab_copies = [send(tab.at[0], tab.at[(-d) % xd], at(dx=d)) for d in range(1, xd)]
        hop = ring(1)
        d_copies = {gi: send_slots(s_d, r_d, gi) for gi in reversed(range(len(groups)))}
        b_copies, c_copies = [], []
        for dy, dc in column:
            there = ((-dc) % cd, (-dy) % yd)
            b_copies.append(send(p_own, pbuf.at[there[0], there[1]], at(dy=dy, dc=dc)))
            c_copies.append(
                send(u_send.at[dc, dy], u_recv.at[there[0], there[1]], at(dy=dy, dc=dc))
            )

        for copy in tab_copies:
            copy.wait_recv()
        peer_tab = pltpu.make_async_copy(tab.at[1:xd], tabs.at[1:xd], lsem.at[8])
        peer_tab.start()
        peer_tab.wait()

        def answer(gi):
            for dx in range(xd):
                for zi in groups[gi]:
                    for j in range(MOST):
                        r = tabs[dx, 1, ((-dx) % xd) * per_x + zi * MOST + j]
                        buf = r_a if dx == 0 else s_a
                        buf[dx * per_x + zi * MOST + j] = zbuf[zi][r]
            return send_slots(s_a, r_a, gi)

        def near_pairs(lo, hi):
            terms = []
            for k in range(lo, hi):
                f, s = np_s[0, k] % CPD, np_s[1, k] % CPD
                terms.append((f, dot_nn(x3[s], nea[k])))
                terms.append((s, dot_nt(x3[f], nea[k])))
            for i in range(CPD):
                nacc[i] = add_where(nacc[i], terms, i)

        def gather_returned(gi):
            for copy in d_copies[gi]:
                copy.wait_recv()
            out = []
            for zi in groups[gi]:
                terms = []
                for dx in range(xd):
                    if zi == 0 and dx == 0:
                        continue
                    for j in range(MOST):
                        s = ((-dx) % xd) * per_x + zi * MOST + j
                        term = r_d[dx * per_x + zi * MOST + j].astype(F32)
                        terms.append((tabs[dx, 1, s], term))
                for i in range(CPD):
                    acc = add_where(jnp.zeros(terms[0][1].shape, F32), terms, i)
                    if zi == 0:
                        d_own[i] = acc
                    else:
                        zsend[zi, i] = acc.astype(BF16)
                if zi:
                    dz = dz_of[zi]
                    out.append(send(zsend.at[zi], zrecv.at[zi_of(-dz)], at(dz=dz)))
            return out

        def first_terms(gi):
            for copy in a_copies[gi]:
                copy.wait_recv()
            terms = []
            for zi in groups[gi]:
                for dx in range(xd):
                    if zi == 0 and dx == 0:
                        continue
                    for j in range(MOST):
                        s = dx * per_x + zi * MOST + j
                        terms.append((tabs[0, 2, s], dot_nn(r_a[s], cou[tabs[0, 3, s]])))
            for i in range(CPD):
                lacc[i] = add_where(lacc[i], terms, i)

        for i in range(CPD):
            lacc[i] = jnp.zeros_like(lacc[i])
        a_copies = {0: answer(0)}
        loads["sel"].wait()
        for i in range(CPD):
            nacc[i] = dot_nn(x3[i], sel[i])
        z_copies = gather_returned(len(groups) - 1)
        loads["nea"].wait()
        mid = near_count // 2
        for h in range(1, half + 1):
            for copy in hop:
                copy.wait_recv()
            if h < half:
                hop = ring(h + 1)
            a_copies[h] = answer(h)
            z_copies += gather_returned(len(groups) - 1 - h)
            if h == 1:
                near_pairs(0, mid)
            elif h == 2:
                near_pairs(mid, near_count)
            else:
                first_terms(h - 3)

        for copy in b_copies + c_copies:
            copy.wait_recv()
        v_terms = [
            (u_first[k], dot_nn(pbuf[u_dc[k], u_dy[k], u_row[k]], uco[k]))
            for k in range(upper_count)
        ]
        for p in range(P1D):
            acc = jnp.zeros(v_terms[0][1].shape, F32)
            for dy, dc in column:
                acc = acc + u_recv[dc, dy, p].astype(F32)
            pf[p] = add_where(acc, v_terms, p).astype(BF16)
        for gi in range(half - 2, half):
            first_terms(gi)
        for copy in z_copies:
            copy.wait_recv()
        for i in range(CPD):
            acc = lacc[i] + d_own[i] + dot_nt(pf[par_s[i] % P1D], tra[i])
            for zi in range(1, zd):
                acc = acc + zrecv[zi, i].astype(F32)
            lacc[i] = acc

        first_terms(half)
        for i in range(CPD):
            total = lacc[i].astype(BF16)
            out_ref[:, i * width:(i + 1) * width] = (nacc[i] + dot_nt(total, bas[i])).astype(BF16)
        for copy in sent:
            copy.wait_send()

    n_sems = (xd - 1) + 2 * half + 2 * len(column) + 2 * (xd - 1) * len(groups) + (zd - 1)
    return kernel, n_sems, xd * per_x


def solution(mesh):
    yd = mesh.shape["branch"] // CORES
    zd = mesh.shape["leaf"] // XDIM
    kernel, n_sems, nslots = make_kernel(yd, zd)

    def on_device(
        vectors, leaf_cluster_bases, transfers, parents, leaf_pairs, live_pairs, couplings,
        upper_pairs, upper_coupling_matrices, self_blocks, near_pairs, near_blocks,
    ):
        nv = vectors.shape[0]
        leaf, k = leaf_cluster_bases.shape[1:]
        any_ = pl.BlockSpec(memory_space=pl.ANY)
        smem = pl.BlockSpec(memory_space=pltpu.SMEM)
        vmem = pl.BlockSpec(memory_space=pltpu.VMEM)
        vm = pltpu.VMEM
        block = (nv, k)
        return pl.pallas_call(
            kernel,
            out_shape=jax.ShapeDtypeStruct(vectors.shape, BF16),
            in_specs=[any_, any_, any_, smem, vmem, smem, any_, smem, any_, any_, smem, any_],
            out_specs=vmem,
            scratch_shapes=[
                vm(vectors.shape, BF16), vm(leaf_cluster_bases.shape, BF16),
                vm(transfers.shape, BF16), vm(couplings.shape, BF16),
                vm(upper_coupling_matrices.shape, BF16), vm(self_blocks.shape, BF16),
                vm(near_blocks.shape, BF16),
                vm((XDIM, 8, LANES), jnp.int32), pltpu.SMEM((XDIM, 8, LANES), jnp.int32),
                vm((P1D,) + block, BF16),
                vm((nslots,) + block, BF16), vm((nslots,) + block, BF16),
                vm((nslots,) + block, BF16), vm((nslots,) + block, BF16),
                vm((couplings.shape[0] + 1,) + block, BF16),
                vm((zd, CPD) + block, BF16), vm((zd, CPD) + block, BF16),
                vm((CPD,) + block, F32),
                vm((CORES, yd, P1D) + block, BF16), vm((CORES, yd, P1D) + block, BF16),
                vm((CORES, yd, P1D) + block, BF16), vm((P1D,) + block, BF16),
                vm((CPD, nv, leaf), BF16), vm((CPD, nv, leaf), F32), vm((CPD,) + block, F32),
                pltpu.SemaphoreType.DMA((9,)),
                pltpu.SemaphoreType.DMA((n_sems,)), pltpu.SemaphoreType.DMA((n_sems,)),
            ] + [vm((CPD,) + block, BF16)] * zd,
            compiler_params=pltpu.CompilerParams(
                collective_id=0, has_side_effects=True, vmem_limit_bytes=56 * 1024 * 1024
            ),
            name="h2_apply",
        )(
            vectors, leaf_cluster_bases, transfers, parents, leaf_pairs.T, live_pairs, couplings,
            upper_pairs.T, upper_coupling_matrices, self_blocks, near_pairs.T, near_blocks,
        )

    both = ("branch", "leaf")
    return jax.shard_map(
        on_device,
        mesh=mesh,
        in_specs=(
            P(None, both), P(both, None, None), P(both, None, None), P(both), P(both, None),
            P(both), P(both, None, None), P(both, None), P(both, None, None),
            P(both, None, None), P(both, None), P(both, None, None),
        ),
        out_specs=P(None, both),
        check_vma=False,
    )
```

time: 319 us -> 41.5 us (0.13)
  the two profiles are of different devices: /device:TPU:16 before, /device:TPU:2 now
where the time goes in v1:
time: 41.5 us; the launch traced here: 41.3 us
  Pallas kernels  39.1 us (94%)
  local copies, waits for them, and re-layouts  1.54 us (4%)
  between operations  0.66 us (2%)
    pallas_call x1, Pallas kernels, on_device(): pl.pallas_call(kernel, out_shape=jax.ShapeDtypeStruct(vectors.shape, BF16...  39.1 us
    unnamed x1, local copies, waits for them, and re-layouts  1.54 us

profile of v1, /device:TPU:2, one launch (start us, length us, event | category | flops | bytes accessed | tf_op | source)
XLA Modules:
  0.0 41.3 jit_solution(114027537829132347)
XLA Ops:
  0.7 39.1 %h2_apply.1 = bf16[32,1536]{1,0:T(8,128)(2,1)} custom-call(bf16[32,1536]{1,0:T(8,128)(2,1)} %vec_h.1, bf16[6,256,128]{2,1,0:T(8,128)(2,1)} %bas_h.1, bf16[6,128,128]{2,1,0:T(8,128)(2,1)} %tra_h.1, s32[6]{0:T(128)} %par_s.1, s32[2,32]{1,0:T(2,128)} %bitcast.3, s32[1]{0:T(128)S(6)} %copy.14.live_s, bf16[32,128,128]{2,1,0:T(8,128)(2,1)} %cou_h.1, ...), custom_call_target="tpu_custom_call" | custom-call | tf_op jit(solution)/shard_map/h2_apply/pallas_call | solution.py:357
  39.8 1.5 %copy.15 = bf16[32,1536]{1,0:T(8,128)(2,1)} copy(bf16[32,1536]{1,0:T(8,128)(2,1)} %h2_apply.1) | data formatting | bytes 196608

commit v2 on v1

--- a/solution.py
+++ b/solution.py
@@ -30,6 +30,8 @@
     cd, xd = CORES, XDIM
     per_x = zd * MOST
     half = zd // 2
+    cut = CPD // 2
+    assert zd == 8
 
     def zi_of(dz):
         dz %= zd
@@ -37,18 +39,16 @@
             return 0
         return 2 * dz - 1 if dz <= half else 2 * (zd - dz)
 
-    dz_of = [0] * zd
-    for d in range(zd):
-        dz_of[zi_of(d)] = d
-    groups = [[0]] + [[2 * h - 1, 2 * h] for h in range(1, half)] + [[zd - 1]]
+    ask_groups = [[0], [1, 2, 3, 4], [5, 6, 7]]
+    back_groups = [[0, 1, 2], [3, 4], [5, 6, 7]]
     column = [(dy, dc) for dc in range(cd) for dy in range(yd) if dy or dc]
 
     def kernel(
-        vec_h, bas_h, tra_h, par_s, lp_v, live_s, cou_h, up_s, uco_h, sel_h, np_s, nea_h,
+        vec_h, bas_h, tra_h, par_s, lp_v, live_v, cou_h, up_s, uco_h, sel_h, np_s, nea_h,
         out_ref,
         vec, bas, tra, cou, uco, sel, nea,
-        tab, tabs, p_own, s_a, r_a, s_d, r_d, t_buf, zsend, zrecv, d_own,
-        pbuf, u_send, u_recv, pf,
+        tab, tabs, p_own, s_a, r_a, s_d, r_d, t_buf, zsend, zrecv, zin, d_own,
+        up_send, up_recv, pf,
         x3, nacc, lacc,
         lsem, ssem, rsem, *zbuf,
     ):
@@ -98,7 +98,7 @@
                 acc = acc + jnp.where(where == i, term, 0.0)
             return acc
 
-        live = live_s[0]
+        live = live_v[...]
         first = lp_v[0:1, :] % CPD
         second = lp_v[1:2, :] % (zd * xd * CPD)
         owner = (second * 10923) >> 16
@@ -150,7 +150,8 @@
         for p in range(P1D):
             acc = add_where(jnp.zeros(lifted[0][1].shape, F32), lifted, p).astype(BF16)
             p_own[p] = acc
-            pbuf[0, 0, p] = acc
+            for dy, dc in column:
+                up_send[dc, dy, p] = acc
 
         loads["cou"].wait()
         own_tab.wait()
@@ -185,22 +186,12 @@
         for dy, dc in column:
             for p in range(P1D):
                 acc = jnp.zeros(u_terms[0][1].shape, F32)
-                u_send[dc, dy, p] = add_where(acc, u_terms, (dc * yd + dy) * P1D + p).astype(BF16)
+                up_send[dc, dy, P1D + p] = add_where(acc, u_terms, (dc * yd + dy) * P1D + p).astype(BF16)
 
         pl.semaphore_wait(barrier, len(partners))
 
-        def ring(h):
-            if h < half:
-                src_l, dst_l = zbuf[zi_of(h - 1)], zbuf[zi_of(h)]
-                src_r, dst_r = zbuf[zi_of(1 - h)], zbuf[zi_of(-h)]
-            else:
-                cut = CPD // 2
-                src_l, dst_l = zbuf[zi_of(h - 1)].at[0:cut], zbuf[zi_of(h)].at[0:cut]
-                src_r, dst_r = zbuf[zi_of(1 - h)].at[cut:CPD], zbuf[zi_of(-h)].at[cut:CPD]
-            return [send(src_l, dst_l, at(dz=-1)), send(src_r, dst_r, at(dz=1))]
-
-        def send_slots(src, dst, gi):
-            lo, n = groups[gi][0] * MOST, len(groups[gi]) * MOST
+        def send_slots(src, dst, group):
+            lo, n = group[0] * MOST, len(group) * MOST
             return [
                 send(
                     src.at[pl.ds(dx * per_x + lo, n)],
@@ -210,16 +201,19 @@
                 for dx in range(1, xd)
             ]
 
+        near_z = {d: send(zbuf[0], zbuf[zi_of(-d)], at(dz=d)) for d in (2, -2, 1, -1)}
         tab_copies = [send(tab.at[0], tab.at[(-d) % xd], at(dx=d)) for d in range(1, xd)]
-        hop = ring(1)
-        d_copies = {gi: send_slots(s_d, r_d, gi) for gi in reversed(range(len(groups)))}
-        b_copies, c_copies = [], []
-        for dy, dc in column:
-            there = ((-dc) % cd, (-dy) % yd)
-            b_copies.append(send(p_own, pbuf.at[there[0], there[1]], at(dy=dy, dc=dc)))
-            c_copies.append(
-                send(u_send.at[dc, dy], u_recv.at[there[0], there[1]], at(dy=dy, dc=dc))
-            )
+        back_copies = {gi: send_slots(s_d, r_d, back_groups[gi]) for gi in (2, 1, 0)}
+        up_copies = [
+            send(up_send.at[dc, dy], up_recv.at[(-dc) % cd, (-dy) % yd], at(dy=dy, dc=dc))
+            for dy, dc in column
+        ]
+
+        for i in range(CPD):
+            lacc[i] = jnp.zeros_like(lacc[i])
+        loads["sel"].wait()
+        for i in range(CPD):
+            nacc[i] = dot_nn(x3[i], sel[i])
 
         for copy in tab_copies:
             copy.wait_recv()
@@ -229,12 +223,12 @@
 
         def answer(gi):
             for dx in range(xd):
-                for zi in groups[gi]:
+                for zi in ask_groups[gi]:
                     for j in range(MOST):
                         r = tabs[dx, 1, ((-dx) % xd) * per_x + zi * MOST + j]
                         buf = r_a if dx == 0 else s_a
                         buf[dx * per_x + zi * MOST + j] = zbuf[zi][r]
-            return send_slots(s_a, r_a, gi)
+            return send_slots(s_a, r_a, ask_groups[gi])
 
         def near_pairs(lo, hi):
             terms = []
@@ -245,35 +239,22 @@
             for i in range(CPD):
                 nacc[i] = add_where(nacc[i], terms, i)
 
-        def gather_returned(gi):
-            for copy in d_copies[gi]:
-                copy.wait_recv()
-            out = []
-            for zi in groups[gi]:
-                terms = []
-                for dx in range(xd):
-                    if zi == 0 and dx == 0:
-                        continue
-                    for j in range(MOST):
-                        s = ((-dx) % xd) * per_x + zi * MOST + j
-                        term = r_d[dx * per_x + zi * MOST + j].astype(F32)
-                        terms.append((tabs[dx, 1, s], term))
-                for i in range(CPD):
-                    acc = add_where(jnp.zeros(terms[0][1].shape, F32), terms, i)
-                    if zi == 0:
-                        d_own[i] = acc
-                    else:
-                        zsend[zi, i] = acc.astype(BF16)
-                if zi:
-                    dz = dz_of[zi]
-                    out.append(send(zsend.at[zi], zrecv.at[zi_of(-dz)], at(dz=dz)))
-            return out
+        def returned(zi):
+            terms = []
+            for dx in range(xd):
+                if zi == 0 and dx == 0:
+                    continue
+                for j in range(MOST):
+                    s = ((-dx) % xd) * per_x + zi * MOST + j
+                    term = r_d[dx * per_x + zi * MOST + j].astype(F32)
+                    terms.append((tabs[dx, 1, s], term))
+            return [add_where(jnp.zeros(terms[0][1].shape, F32), terms, i) for i in range(CPD)]
 
         def first_terms(gi):
-            for copy in a_copies[gi]:
+            for copy in ask_copies[gi]:
                 copy.wait_recv()
             terms = []
-            for zi in groups[gi]:
+            for zi in ask_groups[gi]:
                 for dx in range(xd):
                     if zi == 0 and dx == 0:
                         continue
@@ -283,58 +264,96 @@
             for i in range(CPD):
                 lacc[i] = add_where(lacc[i], terms, i)
 
-        for i in range(CPD):
-            lacc[i] = jnp.zeros_like(lacc[i])
-        a_copies = {0: answer(0)}
-        loads["sel"].wait()
-        for i in range(CPD):
-            nacc[i] = dot_nn(x3[i], sel[i])
-        z_copies = gather_returned(len(groups) - 1)
+        ask_copies = [answer(0)]
+
+        far_z = []
+        for d in (2, -2):
+            near_z[-d].wait_recv()
+            unit = d // 2
+            block = zbuf[zi_of(d)]
+            lo, hi = (0, cut) if d > 0 else (cut, CPD)
+            far_z.append(send(block, zbuf[zi_of(d + unit)], at(dz=-unit)))
+            far_z.append(send(block.at[lo:hi], zbuf[zi_of(2 * d)].at[lo:hi], at(dz=-d)))
+
+        for copy in back_copies[2]:
+            copy.wait_recv()
+        mid_z = {}
+        for d in (3, -3, 4):
+            for i, acc in enumerate(returned(zi_of(d))):
+                zsend[zi_of(d), i] = acc.astype(BF16)
+            if d != 4:
+                unit = 1 if d > 0 else -1
+                mid_z[d] = [send(zsend.at[zi_of(d)], zin.at[zi_of(d)], at(dz=unit))]
+        for unit, lo, hi in ((1, cut, CPD), (-1, 0, cut)):
+            mid_z[3 * unit].append(
+                send(zsend.at[zi_of(4), lo:hi], zin.at[zi_of(4), lo:hi], at(dz=2 * unit))
+            )
+
+        for d in (1, -1):
+            near_z[-d].wait_recv()
+        ask_copies.append(answer(1))
+
         loads["nea"].wait()
-        mid = near_count // 2
-        for h in range(1, half + 1):
-            for copy in hop:
+        near_pairs(0, near_count // 2)
+
+        for copy in back_copies[1]:
+            copy.wait_recv()
+        last_z = []
+        for unit, lo, hi in ((1, cut, CPD), (-1, 0, cut)):
+            for copy in mid_z[3 * unit]:
                 copy.wait_recv()
-            if h < half:
-                hop = ring(h + 1)
-            a_copies[h] = answer(h)
-            z_copies += gather_returned(len(groups) - 1 - h)
-            if h == 1:
-                near_pairs(0, mid)
-            elif h == 2:
-                near_pairs(mid, near_count)
-            else:
-                first_terms(h - 3)
-
-        for copy in b_copies + c_copies:
+            zi = zi_of(2 * unit)
+            for i, acc in enumerate(returned(zi)):
+                acc = acc + zin[zi_of(3 * unit), i].astype(F32)
+                if lo <= i < hi:
+                    acc = acc + zin[zi_of(4), i].astype(F32)
+                zsend[zi, i] = acc.astype(BF16)
+            last_z.append(send(zsend.at[zi], zrecv.at[zi_of(-2 * unit)], at(dz=2 * unit)))
+        for copy in back_copies[0]:
+            copy.wait_recv()
+        for d in (1, -1):
+            zi = zi_of(d)
+            for i, acc in enumerate(returned(zi)):
+                zsend[zi, i] = acc.astype(BF16)
+            last_z.append(send(zsend.at[zi], zrecv.at[zi_of(-d)], at(dz=d)))
+        for i, acc in enumerate(returned(0)):
+            d_own[i] = acc
+
+        for copy in far_z:
+            copy.wait_recv()
+        ask_copies.append(answer(2))
+        near_pairs(near_count // 2, near_count)
+        first_terms(0)
+        first_terms(1)
+
+        for copy in up_copies:
             copy.wait_recv()
         v_terms = [
-            (u_first[k], dot_nn(pbuf[u_dc[k], u_dy[k], u_row[k]], uco[k]))
+            (u_first[k], dot_nn(up_recv[u_dc[k], u_dy[k], u_row[k]], uco[k]))
             for k in range(upper_count)
         ]
         for p in range(P1D):
             acc = jnp.zeros(v_terms[0][1].shape, F32)
             for dy, dc in column:
-                acc = acc + u_recv[dc, dy, p].astype(F32)
+                acc = acc + up_recv[dc, dy, P1D + p].astype(F32)
             pf[p] = add_where(acc, v_terms, p).astype(BF16)
-        for gi in range(half - 2, half):
-            first_terms(gi)
-        for copy in z_copies:
+        lowered = [dot_nt(pf[par_s[i] % P1D], tra[i]) for i in range(CPD)]
+        for copy in last_z:
             copy.wait_recv()
         for i in range(CPD):
-            acc = lacc[i] + d_own[i] + dot_nt(pf[par_s[i] % P1D], tra[i])
-            for zi in range(1, zd):
+            acc = lacc[i] + d_own[i] + lowered[i]
+            for zi in range(1, 5):
                 acc = acc + zrecv[zi, i].astype(F32)
             lacc[i] = acc
 
-        first_terms(half)
+        first_terms(2)
         for i in range(CPD):
             total = lacc[i].astype(BF16)
             out_ref[:, i * width:(i + 1) * width] = (nacc[i] + dot_nt(total, bas[i])).astype(BF16)
         for copy in sent:
             copy.wait_send()
 
-    n_sems = (xd - 1) + 2 * half + 2 * len(column) + 2 * (xd - 1) * len(groups) + (zd - 1)
+    n_sems = 8 + 8 + len(column) + (xd - 1) * (1 + len(ask_groups) + len(back_groups))
     return kernel, n_sems, xd * per_x
 
 
@@ -356,8 +375,8 @@
         block = (nv, k)
         return pl.pallas_call(
             kernel,
-            out_shape=jax.ShapeDtypeStruct(vectors.shape, BF16),
-            in_specs=[any_, any_, any_, smem, vmem, smem, any_, smem, any_, any_, smem, any_],
+            out_shape=pltpu.VMEM(vectors.shape, BF16),
+            in_specs=[any_, any_, any_, smem, vmem, vmem, any_, smem, any_, any_, smem, any_],
             out_specs=vmem,
             scratch_shapes=[
                 vm(vectors.shape, BF16), vm(leaf_cluster_bases.shape, BF16),
@@ -370,9 +389,9 @@
                 vm((nslots,) + block, BF16), vm((nslots,) + block, BF16),
                 vm((couplings.shape[0] + 1,) + block, BF16),
                 vm((zd, CPD) + block, BF16), vm((zd, CPD) + block, BF16),
-                vm((CPD,) + block, F32),
-                vm((CORES, yd, P1D) + block, BF16), vm((CORES, yd, P1D) + block, BF16),
-                vm((CORES, yd, P1D) + block, BF16), vm((P1D,) + block, BF16),
+                vm((zd, CPD) + block, BF16), vm((CPD,) + block, F32),
+                vm((CORES, yd, 2 * P1D) + block, BF16), vm((CORES, yd, 2 * P1D) + block, BF16),
+                vm((P1D,) + block, BF16),
                 vm((CPD, nv, leaf), BF16), vm((CPD, nv, leaf), F32), vm((CPD,) + block, F32),
                 pltpu.SemaphoreType.DMA((9,)),
                 pltpu.SemaphoreType.DMA((n_sems,)), pltpu.SemaphoreType.DMA((n_sems,)),
@@ -382,7 +401,7 @@
             ),
             name="h2_apply",
         )(
-            vectors, leaf_cluster_bases, transfers, parents, leaf_pairs.T, live_pairs, couplings,
+            vectors, leaf_cluster_bases, transfers, parents, leaf_pairs.T, live_pairs.reshape(1, 1), couplings,
             upper_pairs.T, upper_coupling_matrices, self_blocks, near_pairs.T, near_blocks,
         )
 

time: 41.5 us -> 33.8 us (0.81)
  Pallas kernels: 39.1 us -> 32.4 us
  local copies, waits for them, and re-layouts: 1.54 us -> 0.64 us
    pallas_call x1, Pallas kernels: 39.1 us -> 32.4 us  [on_device(): pl.pallas_call(kernel, out_shape=pltpu.VMEM(vectors.shape, BF16), in_spec...]
    unnamed x1, local copies, waits for them, and re-layouts: 1.54 us -> 0.64 us
where the time goes in v2:
time: 33.8 us; the launch traced here: 33.7 us
  Pallas kernels  32.4 us (96%)
  between operations  0.66 us (2%)
  local copies, waits for them, and re-layouts  0.64 us (2%)
    pallas_call x1, Pallas kernels, on_device(): pl.pallas_call(kernel, out_shape=pltpu.VMEM(vectors.shape, BF16), in_spec...  32.4 us

profile of v2, /device:TPU:2, one launch (start us, length us, event | category | flops | bytes accessed | tf_op | source)
XLA Modules:
  0.0 33.7 jit_solution(8258975293581017017)
XLA Ops:
  0.7 32.4 %h2_apply.1 = bf16[32,1536]{1,0:T(8,128)(2,1)S(1)} custom-call(bf16[32,1536]{1,0:T(8,128)(2,1)} %vec_h.1, bf16[6,256,128]{2,1,0:T(8,128)(2,1)} %bas_h.1, bf16[6,128,128]{2,1,0:T(8,128)(2,1)} %tra_h.1, s32[6]{0:T(128)} %par_s.1, s32[2,32]{1,0:T(2,128)} %bitcast.5, s32[1,1]{1,0:T(1,128)} %bitcast.4.live_v, bf16[32,128,128]{2,1,0:T(8,128)(2,1)} %cou_h.1, ...), custom_call_target="tpu_custom_call" | custom-call | tf_op jit(solution)/shard_map/h2_apply/pallas_call | solution.py:376
  33.1 0.6 %copy.14 = bf16[32,1536]{1,0:T(8,128)(2,1)} copy(bf16[32,1536]{1,0:T(8,128)(2,1)S(1)} %h2_apply.1) | data formatting | bytes 196608

commit v3 on v2

--- a/solution.py
+++ b/solution.py
@@ -1,3 +1,5 @@
+import functools
+
 import jax
 import jax.numpy as jnp
 from jax import lax
@@ -41,16 +43,16 @@
 
     ask_groups = [[0], [1, 2, 3, 4], [5, 6, 7]]
     back_groups = [[0, 1, 2], [3, 4], [5, 6, 7]]
-    column = [(dy, dc) for dc in range(cd) for dy in range(yd) if dy or dc]
+    column = [(dy, 0) for dy in range(1, yd)] + [(0, 1)]
 
     def kernel(
         vec_h, bas_h, tra_h, par_s, lp_v, live_v, cou_h, up_s, uco_h, sel_h, np_s, nea_h,
         out_ref,
         vec, bas, tra, cou, uco, sel, nea,
         tab, tabs, p_own, s_a, r_a, s_d, r_d, t_buf, zsend, zrecv, zin, d_own,
-        up_send, up_recv, pf,
+        pbuf, u_send, u_recv, u_acc, c_send, c_recv, pf,
         x3, nacc, lacc,
-        lsem, ssem, rsem, *zbuf,
+        lsem, ssem, rsem, row_ok, col_ok, *zbuf,
     ):
         b = lax.axis_index("branch")
         l = lax.axis_index("leaf")
@@ -65,6 +67,31 @@
             zz, xx = (z + dz) % zd, (x + dx) % xd
             return (yy * cd + cc, zz * xd + xx)
 
+        barrier = pltpu.get_barrier_semaphore()
+        row = [(at(dz=d), (z + d) % zd > z) for d in (1, -1, 2, -2)]
+        row += [(at(dx=d), (x + d) % xd > x) for d in range(1, xd)]
+
+        def turn(yy):
+            return jnp.where(yy < yd // 2, yy, yd + yd // 2 - 1 - yy)
+
+        col = [
+            (at(dy=dy, dc=dc), turn((y + dy) % yd) > turn(y) if dy else c == 0)
+            for dy, dc in column
+        ]
+
+        def signal(sem, device):
+            pl.semaphore_signal(sem, inc=1, device_id=device, device_id_type=MESH)
+
+        def wait_some(sem, amount):
+            pl.when(amount > 0)(lambda: pl.semaphore_wait(sem, amount))
+
+        def number(partners, want_later):
+            flags = [later if want_later else jnp.logical_not(later) for _, later in partners]
+            return sum(jnp.where(flag, 1, 0) for flag in flags)
+
+        for device, later in row + col:
+            pl.when(later)(functools.partial(signal, barrier, device))
+
         loads = {}
         for i, (name, src, dst) in enumerate(
             (("vec", vec_h, vec), ("bas", bas_h, bas), ("tra", tra_h, tra), ("cou", cou_h, cou),
@@ -73,30 +100,33 @@
             loads[name] = pltpu.make_async_copy(src, dst, lsem.at[i])
             loads[name].start()
 
-        barrier = pltpu.get_barrier_semaphore()
-        partners = [at(dz=d) for d in range(1, zd)] + [at(dx=d) for d in range(1, xd)]
-        partners += [at(dy=dy, dc=dc) for dy, dc in column]
-        for device in partners:
-            pl.semaphore_signal(barrier, inc=1, device_id=device, device_id_type=MESH)
-
         count = [0]
         sent = []
 
-        def send(src, dst, device):
+        def ready(src, dst, device):
             i = count[0]
             count[0] += 1
             copy = pltpu.make_async_remote_copy(
                 src_ref=src, dst_ref=dst, send_sem=ssem.at[i], recv_sem=rsem.at[i],
                 device_id=device, device_id_type=MESH,
             )
+            sent.append(copy)
+            return copy
+
+        def send(src, dst, device):
+            copy = ready(src, dst, device)
             copy.start()
-            sent.append(copy)
             return copy
 
         def add_where(acc, terms, i):
             for where, term in terms:
                 acc = acc + jnp.where(where == i, term, 0.0)
             return acc
+
+        wait_some(barrier, number(row + col, False))
+        for sem, partners in ((row_ok, row), (col_ok, col)):
+            for device, later in partners:
+                pl.when(jnp.logical_not(later))(functools.partial(signal, sem, device))
 
         live = live_v[...]
         first = lp_v[0:1, :] % CPD
@@ -145,13 +175,26 @@
             x3[i] = xi
             zbuf[0][i] = dot_nn(xi, bas[i]).astype(BF16)
 
-        loads["tra"].wait()
-        lifted = [(par_s[i] % P1D, dot_nn(zbuf[0][i], tra[i])) for i in range(CPD)]
-        for p in range(P1D):
-            acc = add_where(jnp.zeros(lifted[0][1].shape, F32), lifted, p).astype(BF16)
-            p_own[p] = acc
-            for dy, dc in column:
-                up_send[dc, dy, p] = acc
+        def send_slots(src, dst, group, begin=ready):
+            lo, n = group[0] * MOST, len(group) * MOST
+            return [
+                begin(
+                    src.at[pl.ds(dx * per_x + lo, n)],
+                    dst.at[pl.ds(((-dx) % xd) * per_x + lo, n)],
+                    at(dx=dx),
+                )
+                for dx in range(1, xd)
+            ]
+
+        near_z = {d: ready(zbuf[0], zbuf[zi_of(-d)], at(dz=d)) for d in (2, -2, 1, -1)}
+        tab_copies = [ready(tab.at[0], tab.at[(-d) % xd], at(dx=d)) for d in range(1, xd)]
+
+        def start_row():
+            wait_some(row_ok, number(row, True))
+            for copy in tab_copies + list(near_z.values()):
+                copy.start()
+
+        pl.when(z >= half)(start_row)
 
         loads["cou"].wait()
         own_tab.wait()
@@ -169,6 +212,22 @@
             buf = r_d if dx == 0 else s_d
             for s in range(dx * per_x, (dx + 1) * per_x):
                 buf[s] = t_buf[tabs[0, 0, s]]
+
+        back_copies = {gi: send_slots(s_d, r_d, back_groups[gi]) for gi in (2, 1, 0)}
+
+        def start_back():
+            for gi in (2, 1, 0):
+                for copy in back_copies[gi]:
+                    copy.start()
+
+        pl.when(z >= half)(start_back)
+
+        loads["tra"].wait()
+        lifted = [(par_s[i] % P1D, dot_nn(zbuf[0][i], tra[i])) for i in range(CPD)]
+        for p in range(P1D):
+            acc = add_where(jnp.zeros(lifted[0][1].shape, F32), lifted, p).astype(BF16)
+            p_own[p] = acc
+            pbuf[0, 0, p] = acc
 
         loads["uco"].wait()
         u_first = [up_s[0, k] % P1D for k in range(upper_count)]
@@ -183,31 +242,38 @@
             ((u_dc[k] * yd + u_dy[k]) * P1D + u_row[k], dot_nt(p_own[u_first[k]], uco[k]))
             for k in range(upper_count)
         ]
-        for dy, dc in column:
+        for dy in range(yd):
             for p in range(P1D):
                 acc = jnp.zeros(u_terms[0][1].shape, F32)
-                up_send[dc, dy, P1D + p] = add_where(acc, u_terms, (dc * yd + dy) * P1D + p).astype(BF16)
-
-        pl.semaphore_wait(barrier, len(partners))
-
-        def send_slots(src, dst, group):
-            lo, n = group[0] * MOST, len(group) * MOST
-            return [
-                send(
-                    src.at[pl.ds(dx * per_x + lo, n)],
-                    dst.at[pl.ds(((-dx) % xd) * per_x + lo, n)],
-                    at(dx=dx),
-                )
-                for dx in range(1, xd)
-            ]
-
-        near_z = {d: send(zbuf[0], zbuf[zi_of(-d)], at(dz=d)) for d in (2, -2, 1, -1)}
-        tab_copies = [send(tab.at[0], tab.at[(-d) % xd], at(dx=d)) for d in range(1, xd)]
-        back_copies = {gi: send_slots(s_d, r_d, back_groups[gi]) for gi in (2, 1, 0)}
+                u_send[dy, p] = add_where(acc, u_terms, (yd + dy) * P1D + p).astype(BF16)
+                u_acc[dy, p] = add_where(acc, u_terms, dy * P1D + p)
+        part_copy = ready(u_send, u_recv, at(dc=1))
+        own_copy = ready(p_own, pbuf.at[1, 0], at(dc=1))
         up_copies = [
-            send(up_send.at[dc, dy], up_recv.at[(-dc) % cd, (-dy) % yd], at(dy=dy, dc=dc))
-            for dy, dc in column
+            ready(p_own, pbuf.at[0, (-dy) % yd], at(dy=dy)) for dy in range(1, yd)
         ]
+
+        def start_upper():
+            wait_some(col_ok, number(col, True))
+            for copy in [part_copy, own_copy] + up_copies:
+                copy.start()
+
+        start_upper()
+
+        @pl.when(z < half)
+        def _():
+            start_row()
+            start_back()
+
+
+        far_z = []
+        for d in (2, -2):
+            near_z[-d].wait_recv()
+            unit = d // 2
+            block = zbuf[zi_of(d)]
+            lo, hi = (0, cut) if d > 0 else (cut, CPD)
+            far_z.append(send(block, zbuf[zi_of(d + unit)], at(dz=-unit)))
+            far_z.append(send(block.at[lo:hi], zbuf[zi_of(2 * d)].at[lo:hi], at(dz=-d)))
 
         for i in range(CPD):
             lacc[i] = jnp.zeros_like(lacc[i])
@@ -228,7 +294,7 @@
                         r = tabs[dx, 1, ((-dx) % xd) * per_x + zi * MOST + j]
                         buf = r_a if dx == 0 else s_a
                         buf[dx * per_x + zi * MOST + j] = zbuf[zi][r]
-            return send_slots(s_a, r_a, ask_groups[gi])
+            return send_slots(s_a, r_a, ask_groups[gi], send)
 
         def near_pairs(lo, hi):
             terms = []
@@ -266,15 +332,6 @@
 
         ask_copies = [answer(0)]
 
-        far_z = []
-        for d in (2, -2):
-            near_z[-d].wait_recv()
-            unit = d // 2
-            block = zbuf[zi_of(d)]
-            lo, hi = (0, cut) if d > 0 else (cut, CPD)
-            far_z.append(send(block, zbuf[zi_of(d + unit)], at(dz=-unit)))
-            far_z.append(send(block.at[lo:hi], zbuf[zi_of(2 * d)].at[lo:hi], at(dz=-d)))
-
         for copy in back_copies[2]:
             copy.wait_recv()
         mid_z = {}
@@ -293,8 +350,21 @@
             near_z[-d].wait_recv()
         ask_copies.append(answer(1))
 
-        loads["nea"].wait()
-        near_pairs(0, near_count // 2)
+        part_copy.wait_recv()
+        for dy in range(yd):
+            for p in range(P1D):
+                acc = u_acc[dy, p] + u_recv[dy, p].astype(F32)
+                if dy:
+                    c_send[dy, p] = acc.astype(BF16)
+                else:
+                    u_acc[dy, p] = acc
+        sum_copies = [
+            send(c_send.at[dy], c_recv.at[(-dy) % yd], at(dy=dy)) for dy in range(1, yd)
+        ]
+
+        for copy in far_z:
+            copy.wait_recv()
+        ask_copies.append(answer(2))
 
         for copy in back_copies[1]:
             copy.wait_recv()
@@ -319,41 +389,40 @@
         for i, acc in enumerate(returned(0)):
             d_own[i] = acc
 
-        for copy in far_z:
-            copy.wait_recv()
-        ask_copies.append(answer(2))
+        loads["nea"].wait()
+        near_pairs(0, near_count // 2)
+        for copy in up_copies:
+            copy.wait_recv()
+        share_copy = send(pbuf.at[0, 1:yd], pbuf.at[1, 1:yd], at(dc=1))
         near_pairs(near_count // 2, near_count)
         first_terms(0)
         first_terms(1)
 
-        for copy in up_copies:
+        for copy in [own_copy, share_copy] + sum_copies:
             copy.wait_recv()
         v_terms = [
-            (u_first[k], dot_nn(up_recv[u_dc[k], u_dy[k], u_row[k]], uco[k]))
+            (u_first[k], dot_nn(pbuf[u_dc[k], u_dy[k], u_row[k]], uco[k]))
             for k in range(upper_count)
         ]
         for p in range(P1D):
-            acc = jnp.zeros(v_terms[0][1].shape, F32)
-            for dy, dc in column:
-                acc = acc + up_recv[dc, dy, P1D + p].astype(F32)
+            acc = u_acc[0, p]
+            for dy in range(1, yd):
+                acc = acc + c_recv[dy, p].astype(F32)
             pf[p] = add_where(acc, v_terms, p).astype(BF16)
         lowered = [dot_nt(pf[par_s[i] % P1D], tra[i]) for i in range(CPD)]
+        first_terms(2)
         for copy in last_z:
             copy.wait_recv()
         for i in range(CPD):
             acc = lacc[i] + d_own[i] + lowered[i]
             for zi in range(1, 5):
                 acc = acc + zrecv[zi, i].astype(F32)
-            lacc[i] = acc
-
-        first_terms(2)
-        for i in range(CPD):
-            total = lacc[i].astype(BF16)
+            total = acc.astype(BF16)
             out_ref[:, i * width:(i + 1) * width] = (nacc[i] + dot_nt(total, bas[i])).astype(BF16)
         for copy in sent:
             copy.wait_send()
 
-    n_sems = 8 + 8 + len(column) + (xd - 1) * (1 + len(ask_groups) + len(back_groups))
+    n_sems = 8 + 8 + 2 * yd + 1 + (xd - 1) * (1 + len(ask_groups) + len(back_groups))
     return kernel, n_sems, xd * per_x
 
 
@@ -390,11 +459,15 @@
                 vm((couplings.shape[0] + 1,) + block, BF16),
                 vm((zd, CPD) + block, BF16), vm((zd, CPD) + block, BF16),
                 vm((zd, CPD) + block, BF16), vm((CPD,) + block, F32),
-                vm((CORES, yd, 2 * P1D) + block, BF16), vm((CORES, yd, 2 * P1D) + block, BF16),
+                vm((CORES, yd, P1D) + block, BF16),
+                vm((yd, P1D) + block, BF16), vm((yd, P1D) + block, BF16),
+                vm((yd, P1D) + block, F32),
+                vm((yd, P1D) + block, BF16), vm((yd, P1D) + block, BF16),
                 vm((P1D,) + block, BF16),
                 vm((CPD, nv, leaf), BF16), vm((CPD, nv, leaf), F32), vm((CPD,) + block, F32),
                 pltpu.SemaphoreType.DMA((9,)),
                 pltpu.SemaphoreType.DMA((n_sems,)), pltpu.SemaphoreType.DMA((n_sems,)),
+                pltpu.SemaphoreType.REGULAR, pltpu.SemaphoreType.REGULAR,
             ] + [vm((CPD,) + block, BF16)] * zd,
             compiler_params=pltpu.CompilerParams(
                 collective_id=0, has_side_effects=True, vmem_limit_bytes=56 * 1024 * 1024

time: 33.8 us -> 33.8 us (level)
  the two profiles are of different devices: /device:TPU:2 before, /device:TPU:56 now
where the time goes in v3:
time: 33.8 us; the launch traced here: 33.6 us
  Pallas kernels  32.3 us (96%)
  between operations  0.66 us (2%)
  local copies, waits for them, and re-layouts  0.64 us (2%)
    pallas_call x1, Pallas kernels, on_device(): pl.pallas_call(kernel, out_shape=pltpu.VMEM(vectors.shape, BF16), in_spec...  32.3 us

profile of v3, /device:TPU:56, one launch (start us, length us, event | category | flops | bytes accessed | tf_op | source)
XLA Modules:
  0.0 33.6 jit_solution(15937012422885631605)
XLA Ops:
  0.7 32.3 %h2_apply.1 = bf16[32,1536]{1,0:T(8,128)(2,1)S(1)} custom-call(bf16[32,1536]{1,0:T(8,128)(2,1)} %vec_h.1, bf16[6,256,128]{2,1,0:T(8,128)(2,1)} %bas_h.1, bf16[6,128,128]{2,1,0:T(8,128)(2,1)} %tra_h.1, s32[6]{0:T(128)} %par_s.1, s32[2,32]{1,0:T(2,128)} %bitcast.5, s32[1,1]{1,0:T(1,128)} %bitcast.4.live_v, bf16[32,128,128]{2,1,0:T(8,128)(2,1)} %cou_h.1, ...), custom_call_target="tpu_custom_call" | custom-call | tf_op jit(solution)/shard_map/h2_apply/pallas_call | solution.py:445
  33.0 0.6 %copy.14 = bf16[32,1536]{1,0:T(8,128)(2,1)} copy(bf16[32,1536]{1,0:T(8,128)(2,1)S(1)} %h2_apply.1) | data formatting | bytes 196608
